TPU v7x, 32 devices: a whole 2x2x4 slice. The times are simulated.
32 devices in a mesh: fsdp: 8 (over y, x, core), tensor: 4 (over z).
Axes of the slice: x: 2, y: 2, z: 4, core: 2. Of those that a mesh axis runs over, the one named last changes fastest.
Arguments:
- hidden_t: bfloat16 [28672, 512], P('fsdp', 'tensor'), may hold values from -6 to 6
- down_weight: bfloat16 [28672, 4096], P('fsdp', 'tensor'), may hold values from -0.03125 to 0.03125
- probe: bfloat16 [28672, 4096], P('fsdp', 'tensor'), may hold values from -5 to 5
- grad_moment: bfloat16 [28672, 4096], P('fsdp', 'tensor'), may hold values from -0.0059814453 to 0.0059814453
- curv_moment: bfloat16 [28672, 4096], P('fsdp', 'tensor'), may hold values from 0.0099487305 to 0.099609375
- target: bfloat16 [512, 4096], P('fsdp', 'tensor'), may hold values from -6 to 6
Outputs:
- new_grad_moment: bfloat16 [28672, 4096], P('fsdp', 'tensor')
- new_curv_moment: bfloat16 [28672, 4096], P('fsdp', 'tensor')
- update: bfloat16 [28672, 4096], P('fsdp', 'tensor')
All inputs are finite; a program needn't handle non-finite values.
Results may differ from a plain program's by a relative error of at most 0.0056.
Values may be sent and summed in bfloat16 or wider, within the bound.
A program may use at most 192 MiB of HBM per device.

v0:
```python
import jax
import jax.numpy as jnp
from jax import lax
from jax.sharding import PartitionSpec as P

BETA_ONE = 0.965
BETA_TWO = 0.99
RHO_SCALE = 0.02
EPS_FLOOR = 0.0005


def cotangents(summed, target_rows, col_width, token_count):
    adjoint = ((summed[:, :col_width] - target_rows.astype(jnp.float32)) / token_count).astype(
        jnp.bfloat16
    )
    tangent_adjoint = (summed[:, col_width:] / token_count).astype(jnp.bfloat16)
    return jnp.concatenate([adjoint, tangent_adjoint], axis=1)


def shards(hidden_t, down_weight, probe, grad_moment, curv_moment, target):
    gathered = lax.all_gather(hidden_t, "tensor", axis=1, tiled=True)
    col_width = down_weight.shape[1]
    token_count = gathered.shape[1]
    paired = jnp.concatenate([down_weight, probe], axis=1)
    partial_out = lax.dot_general(
        gathered, paired, (((0,), (0,)), ((), ())), preferred_element_type=jnp.float32
    )
    totals = lax.psum(partial_out, "fsdp")
    target_all = lax.all_gather(target, "fsdp", axis=0, tiled=True)
    stacked = cotangents(totals, target_all, col_width, token_count)
    products = jnp.dot(gathered, stacked, preferred_element_type=jnp.float32)
    gradient = products[:, :col_width]
    hess_probe = products[:, col_width:]
    estimate = probe.astype(jnp.float32) * hess_probe
    moment_next = BETA_ONE * grad_moment.astype(jnp.float32) + (1.0 - BETA_ONE) * gradient
    curv_next = BETA_TWO * curv_moment.astype(jnp.float32) + (1.0 - BETA_TWO) * estimate
    raw_ratio = moment_next / jnp.maximum(RHO_SCALE * curv_next, EPS_FLOOR)
    update = jnp.clip(raw_ratio, -1.0, 1.0)
    return (
        moment_next.astype(jnp.bfloat16),
        curv_next.astype(jnp.bfloat16),
        update.astype(jnp.bfloat16),
    )


def solution(mesh):
    in_specs = (
        P("fsdp", "tensor"),
        P("fsdp", "tensor"),
        P("fsdp", "tensor"),
        P("fsdp", "tensor"),
        P("fsdp", "tensor"),
        P("fsdp", "tensor"),
    )
    out_specs = (P("fsdp", "tensor"), P("fsdp", "tensor"), P("fsdp", "tensor"))
    return jax.shard_map(shards, mesh=mesh, in_specs=in_specs, out_specs=out_specs, check_vma=False)
```

profile of v0, /device:TPU:0, one launch (start us, length us, event | category | flops | bytes accessed | tf_op | source)
XLA Modules:
  0.0 273.3 jit_solution(6230435863053550682)
XLA Ops:
  7.2 0.0 all-gather.3.cloned.1.call-start
  7.2 0.7 all-gather.3.cloned.1.call-update
  7.9 0.0 all-gather.5.cloned.1.call-start
  7.9 0.7 all-gather.5.cloned.1.call-update
  8.6 0.0 all-reduce.2.cloned.1.call-start
  8.7 75.6 %all-gather.3.cloned.1.call-done = bf16[3584,512]{1,0:T(8,128)(2,1)} async-done(((bf16[3584,128]{1,0:T(8,128)(2,1)}), bf16[3584,512]{1,0:T(8,128)(2,1)}) %all-gather.3.cloned.1.call-update) | async-done | bytes 3670032 | tf_op jit(solution)/shard_map/all_gather | solution.py:21
  84.3 16.0 %fusion.8 = f32[512,2048]{0,1:T(8,128)} fusion(bf16[3584,512]{1,0:T(8,128)(2,1)} %all-gather.3.cloned.1.call-done, bf16[3584,1024]{1,0:T(8,128)(2,1)} %param.8, bf16[3584,1024]{1,0:T(8,128)(2,1)} %param.7), kind=kOutput, calls=%fused_computation.12 | convolution fusion | flops 7545552896 | bytes 22544384 | tf_op jit(solution)/shard_map/dot_general | solution.py:25
  100.3 0.0 all-reduce.2.cloned.1.call-update
  100.3 10.2 %copy.19 = bf16[3584,1024]{0,1:T(8,128)(2,1)} copy(bf16[3584,1024]{1,0:T(8,128)(2,1)} %param.8) | data formatting | bytes 14680064 | tf_op args[2]
  110.6 10.2 %copy.16 = bf16[3584,1024]{0,1:T(8,128)(2,1)} copy(bf16[3584,1024]{1,0:T(8,128)(2,1)} %param.9) | data formatting | bytes 14680064 | tf_op args[3]
  120.7 10.0 %copy.18 = bf16[3584,1024]{0,1:T(8,128)(2,1)} copy(bf16[3584,1024]{1,0:T(8,128)(2,1)} %param.10) | data formatting | bytes 14680064 | tf_op args[4]
  130.8 0.0 all-gather.5.cloned.1.call-done
  130.8 1.5 copy.17
  132.3 59.9 %all-reduce.2.cloned.1.call-done = f32[512,2048]{0,1:T(8,128)} async-done(((f32[512,2048]{0,1:T(8,128)}), f32[512,2048]{0,1:T(8,128)}) %all-reduce.2.cloned.1.call-update) | async-done | bytes 4194320 | tf_op jit(solution)/shard_map/psum | solution.py:28
  192.2 0.0 slice-start
  192.2 3.0 %fusion.14 = (bf16[512,1024]{0,1:T(8,128)(2,1)S(1)}, bf16[512,1024]{0,1:T(8,128)(2,1)S(1)}) fusion(f32[512,2048]{0,1:T(8,128)} %all-reduce.2.cloned.1.call-done, bf16[512,1024]{0,1:T(8,128)(2,1)S(1)} %copy.17), kind=kLoop, calls=%fused_computation.18 | loop fusion | flops 3145728 | bytes 7340032 | tf_op jit(solution)/shard_map/convert_element_type | solution.py:13
  195.2 0.0 slice-start.1
  195.3 16.8 %convolution_bitcast_fusion = f32[3584,2048]{0,1:T(8,128)} fusion(bf16[3584,512]{1,0:T(8,128)(2,1)} %all-gather.3.cloned.1.call-done, bf16[512,1024]{0,1:T(8,128)(2,1)S(1)} %get-tuple-element.13, bf16[512,1024]{0,1:T(8,128)(2,1)S(1)} %get-tuple-element.12), kind=kOutput, calls=%fused_computation | convolution fusion | flops 7520387072 | bytes 35127296 | tf_op jit(solution)/shard_map/dot_general | solution.py:31
  212.1 0.0 slice-done
  212.1 0.0 slice-done.1
  212.1 23.6 %clamp_convert_fusion = (bf16[3584,1024]{0,1:T(8,128)(2,1)}, bf16[3584,1024]{0,1:T(8,128)(2,1)}, bf16[3584,1024]{0,1:T(8,128)(2,1)}) fusion(f32[3584,2048]{0,1:T(8,128)} %convolution_bitcast_fusion, bf16[3584,1024]{0,1:T(8,128)(2,1)} %copy.16, bf16[3584,1024]{0,1:T(8,128)(2,1)S(1)} %bitcast.7, bf16[3584,1024]{0,1:T(8,128)(2,1)} %copy.18), kind=kLoop, calls=%fused_computation.10 | loop fusion | flops 62390272 | bytes 73400320 | tf_op jit(solution)/shard_map/convert_element_type | solution.py:42
  235.6 10.4 %copy.20 = bf16[3584,1024]{1,0:T(8,128)(2,1)} copy(bf16[3584,1024]{0,1:T(8,128)(2,1)} %get-tuple-element.11) | data formatting | bytes 14680064
  246.0 10.4 %copy.21 = bf16[3584,1024]{1,0:T(8,128)(2,1)} copy(bf16[3584,1024]{0,1:T(8,128)(2,1)} %get-tuple-element.10) | data formatting | bytes 14680064
  256.4 10.4 %copy.22 = bf16[3584,1024]{1,0:T(8,128)(2,1)} copy(bf16[3584,1024]{0,1:T(8,128)(2,1)} %get-tuple-element.9) | data formatting | bytes 14680064
  (1 shorter events, 0.0 us)
Async XLA Ops:
  7.2 77.1 %all-gather.3.cloned.1.call-start = ((), (), s32[]{:S(2)}) async-start(), calls=%async_computation | async-start | bytes 4587520 | tf_op jit(solution)/shard_map/all_gather | solution.py:21
  7.9 122.9 %all-gather.5.cloned.1.call-start = ((), (), s32[]{:S(2)}) async-start(), calls=%async_computation.2 | async-start | bytes 1179648 | tf_op jit(solution)/shard_map/all_gather | solution.py:29
  8.6 183.6 %all-reduce.2.cloned.1.call-start = ((), (), s32[]{:S(2)}) async-start(), calls=%async_computation.1 | async-start | bytes 8388608 | tf_op jit(solution)/shard_map/psum | solution.py:28
  192.2 19.9 %slice-start = ((s8[7340032]{0:T(1024)(128)(4,1)}), s8[4194304]{0:T(1024)(128)(4,1)S(1)}, s32[]{:S(2)}) async-start(s8[7340032]{0:T(1024)(128)(4,1)} %bitcast.6), calls=%async_computation.3 | async-start | bytes 8388608
  195.2 16.8 %slice-start.1 = ((s8[7340032]{0:T(1024)(128)(4,1)}), s8[3145728]{0:T(1024)(128)(4,1)S(1)}, s32[]{:S(2)}) async-start(s8[7340032]{0:T(1024)(128)(4,1)} %bitcast.6), calls=%async_computation.4 | async-start | bytes 6291456
Sparse Core Ops, SparseCore 0:
  9.6 74.6 all-gather.2
  86.2 21.6 all-gather.4
  111.2 80.9 all-reduce.1
where the time goes:
time: 275 us; the launch traced here: 273 us
  waiting for transfers between devices  137 us (50%)
  local copies, waits for them, and re-layouts  63.2 us (23%)
  matrix products  32.8 us (12%)
  other arithmetic  26.6 us (10%)
  between operations  13.8 us (5%)
    all_gather x1, waiting for transfers between devices, shards(): gathered = lax.all_gather(hidden_t, 'tensor', axis=1, tiled=True)  75.6 us
    unnamed x10, local copies, waits for them, and re-layouts  61.7 us
    psum x1, waiting for transfers between devices, shards(): totals = lax.psum(partial_out, 'fsdp')  59.9 us
    convert_element_type x1, other arithmetic, shards(): update.astype(jnp.bfloat16)  23.6 us
    dot_general x1, matrix products, shards(): products = jnp.dot(gathered, stacked, preferred_element_type=jnp.float32)  16.8 us
    dot_general x1, matrix products, shards(): lax.dot_general(gathered, paired, (((0,), (0,)), ((), ())), preferred_ele...  16 us
  transfers between devices with their start and end apart: 3, of which 2 were waited for; matrix products, arithmetic and copies ran while one was open for 18% of the time, Pallas kernels for 0%

commit v1 on v0

--- a/solution.py
+++ b/solution.py
@@ -18,7 +18,14 @@
 
 
 def shards(hidden_t, down_weight, probe, grad_moment, curv_moment, target):
-    gathered = lax.all_gather(hidden_t, "tensor", axis=1, tiled=True)
+    ring = [hidden_t]
+    for hop in range(3):
+        ring.append(lax.ppermute(ring[-1], "tensor", [(dev, (dev + 1) % 4) for dev in range(4)]))
+    gathered = jnp.roll(
+        jnp.concatenate(ring[::-1], axis=1),
+        (lax.axis_index("tensor") + 1) * ring[0].shape[1],
+        axis=1,
+    )
     col_width = down_weight.shape[1]
     token_count = gathered.shape[1]
     paired = jnp.concatenate([down_weight, probe], axis=1)

time: 275 us -> 236 us (0.86)
  local copies, waits for them, and re-layouts: 63.2 us -> 16 us
  waiting for transfers between devices: 137 us -> 148 us
  matrix products: 32.8 us -> 29.2 us
  starting transfers between devices: 0.11 us -> 3.16 us
    all_gather x1 -> x0, waiting for transfers between devices: 75.6 us -> none  [shards(): gathered = lax.all_gather(hidden_t, 'tensor', axis=1, tiled=True)]
    ppermute x0 -> x3, waiting for transfers between devices: none -> 68.6 us  [shards(): lax.ppermute(ring[-1], 'tensor', [(dev, (dev + 1) % 4) for dev in range(4)])]
    unnamed x10 -> x25, local copies, waits for them, and re-layouts: 61.7 us -> 15.1 us
    psum x1, waiting for transfers between devices: 59.9 us -> 78.9 us  [shards(): totals = lax.psum(partial_out, 'fsdp')]
    ppermute x0 -> x3, starting transfers between devices: none -> 3.08 us  [shards(): lax.ppermute(ring[-1], 'tensor', [(dev, (dev + 1) % 4) for dev in range(4)])]
  transfers between devices with their start and end apart: 3 -> 5, of which waited for: 2 -> 4; matrix products, arithmetic and copies ran while one was open for 18% -> 12% of each run, Pallas kernels for 0% -> 0%
where the time goes in v1:
time: 236 us; the launch traced here: 235 us
  waiting for transfers between devices  148 us (63%)
  matrix products  29.2 us (12%)
  other arithmetic  25.2 us (11%)
  local copies, waits for them, and re-layouts  16 us (7%)
  between operations  14.1 us (6%)
  starting transfers between devices  3.16 us (1%)
    psum x1, waiting for transfers between devices, shards(): totals = lax.psum(partial_out, 'fsdp')  78.9 us
    ppermute x3, waiting for transfers between devices, shards(): lax.ppermute(ring[-1], 'tensor', [(dev, (dev + 1) % 4) for dev in range(4)])  68.6 us
    convert_element_type x1, other arithmetic, shards(): update.astype(jnp.bfloat16)  20.9 us
    dot_general x1, matrix products, shards(): products = jnp.dot(gathered, stacked, preferred_element_type=jnp.float32)  15.5 us
    unnamed x25, local copies, waits for them, and re-layouts  15.1 us
    dot_general x1, matrix products, shards(): lax.dot_general(gathered, paired, (((0,), (0,)), ((), ())), preferred_ele...  13.7 us
  transfers between devices with their start and end apart: 5, of which 4 were waited for; matrix products, arithmetic and copies ran while one was open for 12% of the time, Pallas kernels for 0%

profile of v1, /device:TPU:0, one launch (start us, length us, event | category | flops | bytes accessed | tf_op | source)
XLA Modules:
  0.0 235.3 jit_solution(6145381642236701387)
XLA Ops:
  7.2 0.0 all-gather.2.cloned.1.call-start
  7.2 3.1 %collective-permute-start = (bf16[3584,128]{1,0:T(8,128)(2,1)}, bf16[3584,128]{1,0:T(8,128)(2,1)S(1)}, u32[]{:S(2)}, u32[]{:S(2)}) collective-permute-start(bf16[3584,128]{1,0:T(8,128)(2,1)} %param.6), channel_id=1, source_target_pairs={{0,1},{1,2},{2,3},{3,0},{4,5},{5,6},{6,7},{7,4},{8,9},{9,10},{10,1... | collective-permute-start | bytes 2752520 | tf_op jit(solution)/shard_map/ppermute | solution.py:23
  10.3 22.6 %collective-permute-done = bf16[3584,128]{1,0:T(8,128)(2,1)S(1)} collective-permute-done((bf16[3584,128]{1,0:T(8,128)(2,1)}, bf16[3584,128]{1,0:T(8,128)(2,1)S(1)}, u32[]{:S(2)}, u32[]{:S(2)}) %collective-permute-start) | collective-permute-done | bytes 917536 | tf_op jit(solution)/shard_map/ppermute | solution.py:23
  32.9 0.0 copy-start.1
  32.9 0.9 copy-done.1
  33.8 0.0 collective-permute-start.1
  33.8 23.4 %collective-permute-done.1 = bf16[3584,128]{1,0:T(8,128)(2,1)} collective-permute-done((bf16[3584,128]{1,0:T(8,128)(2,1)S(1)}, bf16[3584,128]{1,0:T(8,128)(2,1)}, u32[]{:S(2)}, u32[]{:S(2)}) %collective-permute-start.1) | collective-permute-done | bytes 917536 | tf_op jit(solution)/shard_map/ppermute | solution.py:23
  57.2 0.0 collective-permute-start.2
  57.2 0.0 all-gather.2.cloned.1.call-update
  57.3 0.0 all-reduce.2.cloned.1.call-start
  57.3 0.0 slice-start
  57.3 0.0 copy-start.2
  57.4 0.0 copy-start
  57.4 22.6 %collective-permute-done.2 = bf16[3584,128]{1,0:T(8,128)(2,1)} collective-permute-done((bf16[3584,128]{1,0:T(8,128)(2,1)}, bf16[3584,128]{1,0:T(8,128)(2,1)}, u32[]{:S(2)}, u32[]{:S(2)}) %collective-permute-start.2) | collective-permute-done | bytes 917536 | tf_op jit(solution)/shard_map/ppermute | solution.py:23
  80.0 2.2 constant_dynamic-update-slice_fusion.7
  82.1 2.2 constant_dynamic-update-slice_fusion.6
  84.3 2.2 constant_dynamic-update-slice_fusion.5
  86.5 0.0 slice-start.1
  86.5 2.3 constant_dynamic-update-slice_fusion.4
  88.8 2.2 constant_dynamic-update-slice_fusion.3
  90.9 2.2 constant_dynamic-update-slice_fusion.2
  93.1 0.0 copy-done.2
  93.1 1.0 constant_dynamic-update-slice_fusion.1
  94.1 0.0 copy-done
  94.1 1.0 constant_dynamic-update-slice_fusion
  95.1 0.0 slice-done
  95.1 0.0 slice-done.1
  95.1 13.7 %fusion.3 = f32[512,2048]{1,0:T(8,128)} fusion(bf16[3584,1024]{1,0:T(8,128)(2,1)S(1)} %bitcast.1, bf16[3584,1024]{1,0:T(8,128)(2,1)} %param.7, bf16[3584,1024]{1,0:T(8,128)(2,1)} %constant_dynamic-update-slice_fusion, s32[]{:T(128)S(6)} %select_n.14), kind=kOutput, calls=%fused_computation.5 | convolution fusion | flops 7545552896 | bytes 22544388 | tf_op jit(solution)/shard_map/dot_general | solution.py:32
  108.8 0.0 all-reduce.2.cloned.1.call-update
  108.8 0.0 all-gather.2.cloned.1.call-done
  108.8 78.9 %all-reduce.2.cloned.1.call-done = f32[512,2048]{1,0:T(8,128)} async-done(((f32[512,2048]{1,0:T(8,128)}), f32[512,2048]{1,0:T(8,128)}) %all-reduce.2.cloned.1.call-update) | async-done | bytes 4194320 | tf_op jit(solution)/shard_map/psum | solution.py:35
  187.7 0.0 slice-start.2
  187.7 0.0 slice-start.4
  187.7 4.3 %fusion.14 = (bf16[512,1024]{1,0:T(8,128)(2,1)S(1)}, bf16[512,1024]{1,0:T(8,128)(2,1)}) fusion(f32[512,2048]{1,0:T(8,128)} %all-reduce.2.cloned.1.call-done, bf16[512,1024]{1,0:T(8,128)(2,1)} %all-gather.2.cloned.1.call-done), kind=kLoop, calls=%fused_computation.19 | loop fusion | flops 3145728 | bytes 7340032 | tf_op jit(solution)/shard_map/convert_element_type | solution.py:13
  192.0 0.0 slice-start.3
  192.0 0.0 slice-start.5
  192.0 15.5 %fusion.8 = f32[3584,2048]{1,0:T(8,128)} fusion(bf16[3584,1024]{1,0:T(8,128)(2,1)} %constant_dynamic-update-slice_fusion, s32[]{:T(128)S(6)} %select_n.14, bf16[512,1024]{1,0:T(8,128)(2,1)} %get-tuple-element.7, bf16[512,1024]{1,0:T(8,128)(2,1)S(1)} %get-tuple-element.6), kind=kOutput, calls=%fused_computation.11 | convolution fusion | flops 7520387072 | bytes 35127300 | tf_op jit(solution)/shard_map/dot_general | solution.py:38
  207.5 0.0 slice-done.2
  207.5 0.0 slice-done.4
  207.5 0.0 slice-done.3
  207.5 0.0 slice-done.5
  207.5 20.9 %clamp_convert_fusion = (bf16[3584,1024]{1,0:T(8,128)(2,1)}, bf16[3584,1024]{1,0:T(8,128)(2,1)}, bf16[3584,1024]{1,0:T(8,128)(2,1)}) fusion(f32[3584,2048]{1,0:T(8,128)} %fusion.8, bf16[3584,1024]{1,0:T(8,128)(2,1)S(1)} %bitcast.5, bf16[3584,1024]{1,0:T(8,128)(2,1)S(1)} %bitcast.3, bf16[3584,1024]{1,0:T(8,128)(2,1)} %param.10), kind=kLoop, calls=%fused_computation.9 | loop fusion | flops 62390272 | bytes 73400320 | tf_op jit(solution)/shard_map/convert_element_type | solution.py:49
  (3 shorter events, 0.0 us)
Async XLA Ops:
  7.2 101.7 %all-gather.2.cloned.1.call-start = ((), (), s32[]{:S(2)}) async-start(), calls=%async_computation.1 | async-start | bytes 1179648 | tf_op jit(solution)/shard_map/all_gather | solution.py:36
  7.2 25.7 %collective-permute-start = (bf16[3584,128]{1,0:T(8,128)(2,1)}, bf16[3584,128]{1,0:T(8,128)(2,1)S(1)}, u32[]{:S(2)}, u32[]{:S(2)}) collective-permute-start(bf16[3584,128]{1,0:T(8,128)(2,1)} %param.6), channel_id=1, source_target_pairs={{0,1},{1,2},{2,3},{3,0},{4,5},{5,6},{6,7},{7,4},{8,9},{9,10},{10,1... | collective-permute-start | bytes 2752520 | tf_op jit(solution)/shard_map/ppermute | solution.py:23
  32.9 0.9 copy-start.1
  33.8 23.4 %collective-permute-start.1 = (bf16[3584,128]{1,0:T(8,128)(2,1)S(1)}, bf16[3584,128]{1,0:T(8,128)(2,1)}, u32[]{:S(2)}, u32[]{:S(2)}) collective-permute-start(bf16[3584,128]{1,0:T(8,128)(2,1)S(1)} %collective-permute-done), channel_id=1, source_target_pairs={{0,1},{1,2},{2,3},{3,0},{4,5},{5,6},{6,7},{7,4},{8,9},{9,10},{10,1... | collective-permute-start | bytes 2752520 | tf_op jit(solution)/shard_map/ppermute | solution.py:23
  57.2 22.7 %collective-permute-start.2 = (bf16[3584,128]{1,0:T(8,128)(2,1)}, bf16[3584,128]{1,0:T(8,128)(2,1)}, u32[]{:S(2)}, u32[]{:S(2)}) collective-permute-start(bf16[3584,128]{1,0:T(8,128)(2,1)} %collective-permute-done.1), channel_id=1, source_target_pairs={{0,1},{1,2},{2,3},{3,0},{4,5},{5,6},{6,7},{7,4},{8,9},{9,10},{10,1... | collective-permute-start | bytes 2752520 | tf_op jit(solution)/shard_map/ppermute | solution.py:23
  57.3 130.5 %all-reduce.2.cloned.1.call-start = ((), (), s32[]{:S(2)}) async-start(), calls=%async_computation | async-start | bytes 8388608 | tf_op jit(solution)/shard_map/psum | solution.py:35
  57.3 37.7 %slice-start = ((s8[7340032]{0:T(1024)(128)(4,1)}), s8[3145728]{0:T(1024)(128)(4,1)S(1)}, s32[]{:S(2)}) async-start(s8[7340032]{0:T(1024)(128)(4,1)} %bitcast), calls=%async_computation.2 | async-start | bytes 6291456
  57.3 35.7 %copy-start.2 = (bf16[3584,128]{1,0:T(8,128)(2,1)S(1)}, bf16[3584,128]{1,0:T(8,128)(2,1)}, u32[]{:S(2)}) copy-start(bf16[3584,128]{1,0:T(8,128)(2,1)} %copy-done.1) | copy-start | bytes 2752516
  57.4 36.7 %copy-start = (bf16[3584,128]{1,0:T(8,128)(2,1)S(1)}, bf16[3584,128]{1,0:T(8,128)(2,1)}, u32[]{:S(2)}) copy-start(bf16[3584,128]{1,0:T(8,128)(2,1)} %param.6) | copy-start | bytes 2752516
  86.5 8.6 %slice-start.1 = ((s8[7340032]{0:T(1024)(128)(4,1)}), s8[4194304]{0:T(1024)(128)(4,1)S(1)}, s32[]{:S(2)}) async-start(s8[7340032]{0:T(1024)(128)(4,1)} %bitcast), calls=%async_computation.3 | async-start | bytes 8388608
  187.7 19.7 %slice-start.2 = ((s8[7340032]{0:T(1024)(128)(4,1)}), s8[4194304]{0:T(1024)(128)(4,1)S(1)}, s32[]{:S(2)}) async-start(s8[7340032]{0:T(1024)(128)(4,1)} %bitcast.2), calls=%async_computation.4 | async-start | bytes 8388608
  187.7 19.7 %slice-start.4 = ((s8[7340032]{0:T(1024)(128)(4,1)}), s8[4194304]{0:T(1024)(128)(4,1)S(1)}, s32[]{:S(2)}) async-start(s8[7340032]{0:T(1024)(128)(4,1)} %bitcast.4), calls=%async_computation.6 | async-start | bytes 8388608
  192.0 15.5 %slice-start.3 = ((s8[7340032]{0:T(1024)(128)(4,1)}), s8[3145728]{0:T(1024)(128)(4,1)S(1)}, s32[]{:S(2)}) async-start(s8[7340032]{0:T(1024)(128)(4,1)} %bitcast.2), calls=%async_computation.5 | async-start | bytes 6291456
  192.0 15.5 %slice-start.5 = ((s8[7340032]{0:T(1024)(128)(4,1)}), s8[3145728]{0:T(1024)(128)(4,1)S(1)}, s32[]{:S(2)}) async-start(s8[7340032]{0:T(1024)(128)(4,1)} %bitcast.4), calls=%async_computation.7 | async-start | bytes 6291456
Sparse Core Ops, SparseCore 0:
  57.4 24.7 all-gather.1
  108.9 78.7 all-reduce.1
